TPU v7x, 256 devices: a whole 4x4x8 slice. The times are simulated.
256 devices in a mesh: dp: 8 (over y, x_lo), context: 8 (over z), tensor: 4 (over x_hi, core).
Axes of the slice: x: 4 (x_hi: 2, x_lo: 2; x = x_hi * 2 + x_lo), y: 4, z: 8, core: 2. Of those that a mesh axis runs over, the one named last changes fastest.
Arguments:
- layer_input: bfloat16 [8, 4096, 8192], P('dp', 'context'), may hold values from -60 to 60
- queries: bfloat16 [8, 4096, 4096], P('dp', 'context', 'tensor'), may hold values from -6 to 6
- rotated_key_states: bfloat16 [8, 4096, 512], P('dp', 'context', 'tensor'), may hold values from -6 to 6
- values: bfloat16 [8, 4096, 512], P('dp', 'context', 'tensor'), may hold values from -6 to 6
- attention_out: bfloat16 [8, 4096, 4096], P('dp', 'context', 'tensor'), may hold values from -6 to 6
- output_grad: bfloat16 [8, 4096, 4096], P('dp', 'context', 'tensor'), may hold values from -6 to 6
- normalizer_shift: float32 [32], P('tensor'), may hold values from 0 to 1.5
- document_lengths: int32 [8, 16], P('dp'), may hold values from 1 to 3072, 4096 in all within a row
- dither: int32 [2, 8192, 512], P(None, ('dp', 'context'), 'tensor'), may hold values from 0 to 255
Outputs:
- query_grad: bfloat16 [8, 4096, 4096], P('dp', 'context', 'tensor')
- weight_codes: float32 [2, 8192, 512], P(None, ('dp', 'context'), 'tensor')
Inputs may be any that keep to these rules, and one draw needn't show every extreme that they name: `document_lengths`: each sequence's lengths sum to 4096, and its longest document has exactly 3072 positions.
All inputs are finite; a program needn't handle non-finite values. Where the computation divides by a largest or mean magnitude, that divisor is 1e-20 or more.
Results may differ from a plain program's by a relative error of at most 0.0064.
Values may be sent and summed in bfloat16 or wider, within the bound.
No kernel may reach another device: no remote copies, remote signals or barrier semaphores. Data moves between devices by JAX's collectives and lax.ppermute only.
A program may use at most 64 MiB of HBM per device.

v0:
```python
import math

import jax
import jax.numpy as jnp
from jax import lax
from jax.sharding import PartitionSpec as P

HEAD_SIZE = 128
CODE_BLOCK_ROWS = 128


def document_tables(boundary, positions):
    document = jnp.sum((positions[:, None] >= boundary[None, :]).astype(jnp.int32), axis=1)
    opening = jnp.max(
        jnp.where(boundary[None, :] <= positions[:, None], boundary[None, :], 0), axis=1
    )
    return (document, opening)


def tile_grads(
    query_row_block,
    gradient_block,
    row_delta,
    log_norm,
    query_index,
    query_segment,
    key_tile_slice,
    value_tile_slice,
    key_index,
    key_segment,
):
    softmax_scale = HEAD_SIZE ** (-0.5)
    scores = (
        jnp.einsum(
            "vfxu,yfu->fxvy", query_row_block, key_tile_slice, preferred_element_type=jnp.float32
        )
        * softmax_scale
    )
    allowed = (key_index[None, :] <= query_index[:, None]) & (
        key_segment[None, :] == query_segment[:, None]
    )
    probabilities = jnp.where(allowed[None, None], jnp.exp(scores - log_norm[:, :, :, None]), 0.0)
    value_portion = jnp.einsum(
        "hyvz,vhyb->zhb",
        probabilities.astype(jnp.bfloat16),
        gradient_block,
        preferred_element_type=jnp.float32,
    )
    prob_grad = jnp.einsum(
        "vfxu,yfu->fxvy", gradient_block, value_tile_slice, preferred_element_type=jnp.float32
    )
    score_gradient = (probabilities * (prob_grad - row_delta[:, :, :, None])).astype(jnp.bfloat16)
    query_part = (
        jnp.einsum(
            "wqan,nwk->awqk", score_gradient, key_tile_slice, preferred_element_type=jnp.float32
        )
        * softmax_scale
    )
    key_portion = (
        jnp.einsum(
            "hyvz,vhyb->zhb", score_gradient, query_row_block, preferred_element_type=jnp.float32
        )
        * softmax_scale
    )
    return (query_part, key_portion, value_portion)


def per_device(
    layer_input,
    queries,
    rotated_key_states,
    values,
    attention_out,
    output_grad,
    normalizer_shift,
    document_lengths,
    dither,
):
    local_rows = queries.shape[1]
    half_rows = local_rows // 2
    context_size = lax.axis_size("context")
    context_rank = lax.axis_index("context")
    seq_length = local_rows * context_size
    kv_heads = rotated_key_states.shape[2] // HEAD_SIZE
    query_group_width = queries.shape[2] // HEAD_SIZE // kv_heads
    boundary = jnp.cumsum(document_lengths[0])
    head_log_offset = normalizer_shift.reshape(kv_heads, query_group_width)
    own_start = context_rank * local_rows
    query_rows = queries[0]
    output_rows = attention_out[0]
    grad_rows = output_grad[0]
    block_start = jnp.stack([own_start, own_start + half_rows])
    block_shape = (2, half_rows, kv_heads, query_group_width, HEAD_SIZE)
    query_rows = query_rows.reshape(block_shape)
    output_rows = output_rows.reshape(block_shape)
    grad_rows = grad_rows.reshape(block_shape)
    row_delta = jnp.sum(
        grad_rows.astype(jnp.float32) * output_rows.astype(jnp.float32), axis=-1
    ).transpose(0, 2, 3, 1)
    query_index = block_start[:, None] + jnp.arange(half_rows, dtype=jnp.int32)[None, :]
    query_segment, opening = document_tables(boundary, query_index.reshape(-1))
    query_segment = query_segment.reshape(2, half_rows)
    opening = opening.reshape(2, half_rows)
    visible = (query_index - opening + 1).astype(jnp.float32)
    log_norm = jnp.log(visible)[:, None, None, :] + head_log_offset[None, :, :, None]
    initial = (
        jnp.zeros(block_shape, jnp.float32),
        jnp.zeros((seq_length, kv_heads, HEAD_SIZE), jnp.float32),
        jnp.zeros((seq_length, kv_heads, HEAD_SIZE), jnp.float32),
    )
    key_piece = lax.all_gather(rotated_key_states, "context", axis=1, tiled=True)[0]
    value_piece = lax.all_gather(values, "context", axis=1, tiled=True)[0]
    piece_rows = key_piece.shape[0]
    tile_rows = math.gcd(piece_rows, local_rows)

    def one_tile(tile_number, state):
        query_acc, key_acc, value_acc = state
        offset = tile_number * tile_rows
        key_tile_slice = lax.dynamic_slice_in_dim(key_piece, offset, tile_rows, 0).reshape(
            tile_rows, kv_heads, HEAD_SIZE
        )
        value_tile_slice = lax.dynamic_slice_in_dim(value_piece, offset, tile_rows, 0).reshape(
            tile_rows, kv_heads, HEAD_SIZE
        )
        key_index = offset + jnp.arange(tile_rows, dtype=jnp.int32)
        key_segment, unused = document_tables(boundary, key_index)
        key_total = jnp.zeros((tile_rows, kv_heads, HEAD_SIZE), jnp.float32)
        value_total = jnp.zeros((tile_rows, kv_heads, HEAD_SIZE), jnp.float32)
        for block in range(2):
            skipped = (offset > block_start[block] + half_rows - 1) | (
                key_segment[tile_rows - 1] < query_segment[block, 0]
            )

            def empty_parts():
                return (
                    jnp.zeros(block_shape[1:], jnp.float32),
                    jnp.zeros((tile_rows, kv_heads, HEAD_SIZE), jnp.float32),
                    jnp.zeros((tile_rows, kv_heads, HEAD_SIZE), jnp.float32),
                )

            def real_parts():
                return tile_grads(
                    query_rows[block],
                    grad_rows[block],
                    row_delta[block],
                    log_norm[block],
                    query_index[block],
                    query_segment[block],
                    key_tile_slice,
                    value_tile_slice,
                    key_index,
                    key_segment,
                )

            query_part, key_portion, value_portion = lax.cond(skipped, empty_parts, real_parts)
            query_acc = query_acc.at[block].add(query_part)
            key_total = key_total + key_portion
            value_total = value_total + value_portion
        key_acc = lax.dynamic_update_slice_in_dim(
            key_acc, lax.dynamic_slice_in_dim(key_acc, offset, tile_rows, 0) + key_total, offset, 0
        )
        value_acc = lax.dynamic_update_slice_in_dim(
            value_acc,
            lax.dynamic_slice_in_dim(value_acc, offset, tile_rows, 0) + value_total,
            offset,
            0,
        )
        return (query_acc, key_acc, value_acc)

    query_acc, key_acc, value_acc = lax.fori_loop(0, piece_rows // tile_rows, one_tile, initial)
    query_grad = query_acc.astype(jnp.bfloat16).reshape(local_rows, -1)
    key_sum, value_sum = (
        lax.psum_scatter(
            key_acc.reshape(seq_length, -1), "context", scatter_dimension=0, tiled=True
        ),
        lax.psum_scatter(
            value_acc.reshape(seq_length, -1), "context", scatter_dimension=0, tiled=True
        ),
    )
    shared_grad = jnp.concatenate(
        [key_sum.astype(jnp.bfloat16), value_sum.astype(jnp.bfloat16)], axis=1
    )
    features = layer_input[0]
    weight_gradient = lax.psum_scatter(
        lax.dot_general(
            features, shared_grad, (((0,), (0,)), ((), ())), preferred_element_type=jnp.float32
        ),
        ("dp", "context"),
        scatter_dimension=0,
        tiled=True,
    )
    own_rows = weight_gradient.shape[0]
    code_blocks = weight_gradient.reshape(
        own_rows // CODE_BLOCK_ROWS, CODE_BLOCK_ROWS, 2, kv_heads, HEAD_SIZE
    )
    largest_value = jnp.max(jnp.abs(code_blocks), axis=(1, 4), keepdims=True)
    scaled_scores = (
        (8.0 * code_blocks / (largest_value + 1e-06))
        .reshape(own_rows, 2, kv_heads * HEAD_SIZE)
        .transpose(1, 0, 2)
    )
    weight_codes = scaled_scores + (dither.astype(jnp.float32) + 0.5) / 256.0
    return (query_grad[None], weight_codes)


def solution(mesh):
    placed = (
        P("dp", "context", None),
        P("dp", "context", "tensor"),
        P("dp", "context", "tensor"),
        P("dp", "context", "tensor"),
        P("dp", "context", "tensor"),
        P("dp", "context", "tensor"),
        P("tensor"),
        P("dp", None),
        P(None, ("dp", "context"), "tensor"),
    )
    return jax.shard_map(
        per_device,
        mesh=mesh,
        in_specs=placed,
        out_specs=(P("dp", "context", "tensor"), P(None, ("dp", "context"), "tensor")),
        check_vma=False,
    )
```

profile of v0, /device:TPU:4, one launch (start us, length us, event | category | flops | bytes accessed | tf_op | source)
XLA Modules:
  0.0 799.2 jit_solution(17825783243404643158)
XLA Ops:
  10.4 1.6 copy.45
  17.4 34.1 %all-gather.3.cloned.1.call-done = bf16[1,4096,128]{2,1,0:T(8,128)(2,1)} async-done(((bf16[1,512,128]{2,1,0:T(8,128)(2,1)}), bf16[1,4096,128]{2,1,0:T(8,128)(2,1)}) %all-gather.3.cloned.1.call-update) | async-done | bytes 1048592 | tf_op jit(solution)/shard_map/all_gather | solution.py:111
  51.5 39.0 %all-gather.5.cloned.1.call-done = bf16[1,4096,128]{2,1,0:T(8,128)(2,1)} async-done(((bf16[1,512,128]{2,1,0:T(8,128)(2,1)}), bf16[1,4096,128]{2,1,0:T(8,128)(2,1)}) %all-gather.5.cloned.1.call-update) | async-done | bytes 1048592 | tf_op jit(solution)/shard_map/all_gather | solution.py:112
  90.7 1.5 broadcast.298
  92.2 1.4 broadcast.298.clone
  93.6 136.6 %while.23 = (s32[]{:T(128)}, f32[2,256,1,8,128]{4,1,3,2,0:T(8,128)S(1)}, f32[4096,1,128]{2,0,1:T(8,128)}, f32[4096,1,128]{2,0,1:T(8,128)}, s32[]{:T(128)}, /*ind...) while((s32[]{:T(128)}, ...), condition=%wide.region_10.11_spmd.clone, body=%wide.region_4.10_spmd.clone.sunk | while | flops 2707583488 | bytes 56786168 | solution.py:170
  94.2 1.3 convert_reduce_fusion.3
  95.5 1.3 slice.245
  101.7 1.6 dynamic-slice_bitcast_fusion.5
  103.3 11.6 %conditional.6 = (f32[512,1,128]{2,0,1:T(8,128)S(1)}, f32[512,1,128]{2,0,1:T(8,128)S(1)}, f32[1,256,1,8,128]{4,1,3,2,0:T(8,128)S(1)}) conditional(s32[]{:T(128)} %convert_element_type.137, (s32[512]{0:T(512)}, s32[2,256]{1,0:T(2,128)}, s32[512]{0:T(512)}, s32[2,256]{1,0:T(2,128)}, bf16[512,1,128]{2,0,1:T(8,128)(2,1)S(1)}, ...), branch_computations={%region_6.6_spmd, %region_7.7_spmd} | conditional | flops 1353383936 | bytes 23398424 | solution.py:155
  103.3 1.7 fusion.38
  107.9 2.5 fusion.5
  110.5 1.7 fusion.32
  112.2 1.9 fusion.23
  116.8 11.6 %conditional.7 = (f32[512,1,128]{2,0,1:T(8,128)S(1)}, f32[512,1,128]{2,0,1:T(8,128)S(1)}, f32[1,256,1,8,128]{4,1,3,2,0:T(8,128)S(1)}) conditional(s32[]{:T(128)} %convert_element_type.138, (s32[512]{0:T(512)}, s32[2,256]{1,0:T(2,128)}, s32[512]{0:T(512)}, s32[2,256]{1,0:T(2,128)}, bf16[512,1,128]{2,0,1:T(8,128)(2,1)S(1)}, ...), branch_computations={%region_8.8_spmd, %region_9.9_spmd} | conditional | flops 1353383936 | bytes 23398424 | solution.py:155
  116.8 1.8 fusion.83
  121.5 2.5 fusion.50
  124.0 1.7 fusion.77
  125.8 1.9 fusion.68
  128.7 2.0 add_dynamic-update-slice_fusion.6
  131.4 1.3 convert_reduce_fusion.3
  132.7 1.3 slice.245
  138.9 1.6 dynamic-slice_bitcast_fusion.5
  143.0 2.0 add_dynamic-update-slice_fusion.6
  145.6 1.3 convert_reduce_fusion.3
  146.9 1.3 slice.245
  153.1 1.6 dynamic-slice_bitcast_fusion.5
  157.2 2.0 add_dynamic-update-slice_fusion.6
  159.8 1.3 convert_reduce_fusion.3
  161.1 1.3 slice.245
  167.3 1.6 dynamic-slice_bitcast_fusion.5
  171.4 2.0 add_dynamic-update-slice_fusion.6
  174.0 1.3 convert_reduce_fusion.3
  175.3 1.3 slice.245
  181.5 1.6 dynamic-slice_bitcast_fusion.5
  185.6 2.0 add_dynamic-update-slice_fusion.6
  188.2 1.3 convert_reduce_fusion.3
  189.5 1.3 slice.245
  195.7 1.6 dynamic-slice_bitcast_fusion.5
  199.8 2.0 add_dynamic-update-slice_fusion.6
  210.0 1.6 dynamic-slice_bitcast_fusion.5
  214.0 2.0 add_dynamic-update-slice_fusion.6
  224.2 1.6 dynamic-slice_bitcast_fusion.5
  228.2 2.0 add_dynamic-update-slice_fusion.6
  231.1 176.2 %reduce-scatter.6.cloned.1.call-done = f32[512,128]{1,0:T(8,128)} async-done(((f32[4096,128]{1,0:T(8,128)}), f32[512,128]{1,0:T(8,128)}) %reduce-scatter.6.cloned.1.call-update) | async-done | bytes 262160 | tf_op jit(solution)/shard_map/reduce_scatter | solution.py:176
  408.3 42.3 %reduce-scatter.4.cloned.1.call-done = f32[512,128]{1,0:T(8,128)} async-done(((f32[4096,128]{1,0:T(8,128)}), f32[512,128]{1,0:T(8,128)}) %reduce-scatter.4.cloned.1.call-update) | async-done | bytes 262160 | tf_op jit(solution)/shard_map/reduce_scatter | solution.py:173
  451.5 9.0 %convolution_bitcast_fusion = f32[8192,256]{0,1:T(8,128)} fusion(bf16[1,512,8192]{2,1,0:T(8,128)(2,1)} %param.19, bf16[512,128]{1,0:T(8,128)(2,1)S(1)} %convert_element_type.107, bf16[512,128]{1,0:T(8,128)(2,1)S(1)} %convert_element_type.106), kind=kOutput, calls=%fused_computation.87 | convolution fusion | flops 2148007936 | bytes 17039360 | tf_op jit(solution)/shard_map/dot_general | solution.py:185
  462.7 328.0 %reduce-scatter.8.cloned.1.call-done = f32[128,256]{0,1:T(8,128)} async-done(((f32[8192,256]{0,1:T(8,128)}), f32[128,256]{0,1:T(8,128)}) %reduce-scatter.8.cloned.1.call-update) | async-done | bytes 131088 | tf_op jit(solution)/shard_map/reduce_scatter | solution.py:184
  (250 shorter events, 72.0 us)
Async XLA Ops:
  7.2 6.0 copy-start.2
  7.2 44.3 %all-gather.3.cloned.1.call-start = ((), (), s32[]{:S(2)}) async-start(), calls=%async_computation.3 | async-start | bytes 1179648 | tf_op jit(solution)/shard_map/all_gather | solution.py:111
  7.9 82.6 %all-gather.5.cloned.1.call-start = ((), (), s32[]{:S(2)}) async-start(), calls=%async_computation.4 | async-start | bytes 1179648 | tf_op jit(solution)/shard_map/all_gather | solution.py:112
  8.7 398.6 %reduce-scatter.6.cloned.1.call-start = ((), (), s32[]{:S(2)}) async-start(), calls=%async_computation.6 | async-start | bytes 2359296 | tf_op jit(solution)/shard_map/reduce_scatter | solution.py:176
  10.4 4.2 copy-start.1
  93.6 6.4 copy-start.4
  93.6 6.4 copy-start.6
  114.9 0.7 copy-start
  128.5 2.3 copy-start.5
  128.5 2.3 copy-start.7
  130.8 6.4 copy-start.4
  130.8 6.4 copy-start.6
  140.6 0.7 copy-start
  142.7 2.3 copy-start.5
  142.7 2.3 copy-start.7
  145.0 6.4 copy-start.4
  145.0 6.4 copy-start.6
  154.8 0.7 copy-start
  156.9 2.3 copy-start.5
  156.9 2.3 copy-start.7
  159.2 6.4 copy-start.4
  159.2 6.4 copy-start.6
  169.0 0.7 copy-start
  171.1 2.3 copy-start.5
  171.1 2.3 copy-start.7
  173.4 6.4 copy-start.4
  173.4 6.4 copy-start.6
  183.2 0.7 copy-start
  185.3 2.3 copy-start.5
  185.3 2.3 copy-start.7
  187.6 6.4 copy-start.4
  187.6 6.4 copy-start.6
  197.4 0.7 copy-start
  199.5 2.3 copy-start.5
  199.6 2.3 copy-start.7
  201.9 6.4 copy-start.4
  201.9 6.4 copy-start.6
  211.7 0.7 copy-start
  213.8 2.3 copy-start.5
  213.8 2.3 copy-start.7
  216.1 6.4 copy-start.4
  216.1 6.4 copy-start.6
  225.9 0.7 copy-start
  228.0 2.3 copy-start.5
  228.0 2.3 copy-start.7
  230.3 220.2 %reduce-scatter.4.cloned.1.call-start = ((), (), s32[]{:S(2)}) async-start(), calls=%async_computation.5 | async-start | bytes 2359296 | tf_op jit(solution)/shard_map/reduce_scatter | solution.py:173
  230.9 559.8 %reduce-scatter.8.cloned.1.call-start = ((), (), s32[]{:S(2)}) async-start(), calls=%async_computation.7 | async-start | bytes 8519680 | tf_op jit(solution)/shard_map/reduce_scatter | solution.py:184
  460.5 331.4 %copy-start.3 = (s32[2,128,128]{2,1,0:T(8,128)S(1)}, s32[2,128,128]{2,1,0:T(8,128)}, u32[]{:S(2)}) copy-start(s32[2,128,128]{2,1,0:T(8,128)} %param.27) | copy-start | bytes 393220
Sparse Core Ops, SparseCore 0:
  9.8 41.6 all-gather.2
  53.3 37.1 all-gather.4
  230.4 176.8 reduce-scatter.5
  409.7 40.8 reduce-scatter.3
  460.6 329.9 reduce-scatter.7
where the time goes:
time: 805 us; the launch traced here: 799 us
  waiting for transfers between devices  621 us (77%)
  local copies, waits for them, and re-layouts  61.3 us (8%)
  other arithmetic  54.1 us (7%)
  matrix products  26.3 us (3%)
  loops' own time  21.8 us (3%)
  between operations  13.9 us (2%)
    reduce_scatter x1, waiting for transfers between devices, per_device(): lax.psum_scatter(lax.dot_general(features, shared_grad, (((0,), (0,)), ((...  328 us
    reduce_scatter x1, waiting for transfers between devices, per_device(): lax.psum_scatter(value_acc.reshape(seq_length, -1), 'context', scatter_di...  176 us
    reduce_scatter x1, waiting for transfers between devices, per_device(): lax.psum_scatter(key_acc.reshape(seq_length, -1), 'context', scatter_dime...  42.3 us
    all_gather x1, waiting for transfers between devices, per_device(): value_piece = lax.all_gather(values, 'context', axis=1, tiled=True)[0]  39 us
    all_gather x1, waiting for transfers between devices, per_device(): lax.all_gather(rotated_key_states, 'context', axis=1, tiled=True)[0]  34.1 us
    another operation x1, loops' own time, per_device(): lax.fori_loop(0, piece_rows // tile_rows, one_tile, initial)  21.4 us
    dynamic_update_slice x8, other arithmetic, one_tile(): lax.dynamic_update_slice_in_dim(value_acc, lax.dynamic_slice_in_dim(value...  16.2 us
  transfers between devices with their start and end apart: 5, of which 5 were waited for; matrix products, arithmetic and copies ran while one was open for 1% of the time, Pallas kernels for 0%

commit v1 on v0

v1 whole, which is shorter than its diff:
```python
import functools
import math

import jax
import jax.numpy as jnp
from jax import lax
from jax.experimental import pallas as pl
from jax.experimental.pallas import tpu as pltpu
from jax.sharding import PartitionSpec as P

HEAD_SIZE = 128
SOFTMAX_SCALE = HEAD_SIZE ** (-0.5)
LOG2_E = math.log2(math.e)
KEY_TILE = 256
VMEM_LIMIT = 40 << 20
F32 = jnp.float32
BF16 = jnp.bfloat16

NT = (((1,), (1,)), ((), ()))
NN = (((1,), (0,)), ((), ()))
TN = (((0,), (0,)), ((), ()))


def dot(a, b, dims):
    return lax.dot_general(a, b, dims, preferred_element_type=F32)


def vmem_params():
    return pltpu.CompilerParams(vmem_limit_bytes=VMEM_LIMIT)


def opening_of(lengths_ref, position):
    total = jnp.int32(0)
    opening = jnp.zeros_like(position)
    for n in range(lengths_ref.shape[1]):
        total = total + lengths_ref[0, n]
        opening = jnp.where(total <= position, total, opening)
    return opening


def attention_body(shifts, first, last, *refs):
    blocks = len(shifts)
    rank_ref, lengths_ref, shift_ref, q_ref, do_ref, second_ref = refs[:6]
    rest = list(refs[6:])
    kv_refs = [rest.pop(0) for _ in range(blocks)]
    dq_in_ref = None if first else rest.pop(0)
    dq_ref = rest.pop(0)
    delta_out_ref = rest.pop(0) if first else None
    dkv_refs = [rest.pop(0) for _ in range(blocks)]
    acc_ref, key_t_ref, opening_ref, log_ref, dq_acc_ref = rest
    head = pl.program_id(0)
    rows = q_ref.shape[0]
    start = rank_ref[0] * rows
    first_opening = opening_of(lengths_ref, start)
    last_opening = opening_of(lengths_ref, start + rows - 1)

    @pl.when(head == 0)
    def _():
        acc_ref[...] = jnp.zeros_like(acc_ref)
        for b in range(blocks):
            key_t_ref[b] = kv_refs[b][:, :HEAD_SIZE].T
        position = start + lax.broadcasted_iota(jnp.int32, (8, rows), 1)
        opening = opening_of(lengths_ref, position)
        opening_ref[...] = opening
        log_ref[...] = jnp.log((position - opening + 1).astype(F32))

    log_norm = (log_ref[0:1, :] + shift_ref[head]) * LOG2_E
    if first:
        product = second_ref[...].astype(F32) * do_ref[...].astype(F32)
        row_delta = jnp.sum(product.T, axis=0, keepdims=True)
        delta_out_ref[0] = row_delta
        dq_acc_ref[...] = jnp.zeros_like(dq_acc_ref)
    else:
        row_delta = second_ref[0]
        dq_acc_ref[...] = dq_in_ref[0]

    def tile(b, k0, q0, masked):
        k = kv_refs[b][k0 : k0 + KEY_TILE, :HEAD_SIZE]
        v = kv_refs[b][k0 : k0 + KEY_TILE, HEAD_SIZE:]
        q = q_ref[q0:, :]
        do = do_ref[q0:, :]
        scores = dot(k, q, NT)
        probs = jnp.exp2(scores * (SOFTMAX_SCALE * LOG2_E) - log_norm[:, q0:])
        if masked:
            key = (start - shifts[b] * rows + k0) + lax.broadcasted_iota(jnp.int32, scores.shape, 0)
            allowed = key >= opening_ref[0:1, q0:]
            if shifts[b] == 0:
                query = (start + q0) + lax.broadcasted_iota(jnp.int32, scores.shape, 1)
                allowed = allowed & (key <= query)
            probs = jnp.where(allowed, probs, 0.0)
        prob_grad = dot(v, do, NT)
        score_grad = (probs * (prob_grad - row_delta[:, q0:])).astype(BF16)
        acc_ref[b, k0 : k0 + KEY_TILE, HEAD_SIZE:] += dot(probs.astype(BF16), do, NN)
        acc_ref[b, k0 : k0 + KEY_TILE, :HEAD_SIZE] += dot(score_grad, q, NN)
        dq_acc_ref[:, q0:] += dot(key_t_ref[b, :, k0 : k0 + KEY_TILE], score_grad, NN)

    for b in range(blocks):
        for k0 in range(0, rows, KEY_TILE):
            if shifts[b] == 0:
                tile(b, k0, k0, True)
                continue
            key_start = start - shifts[b] * rows + k0
            reached = (key_start >= 0) & (first_opening < key_start + KEY_TILE)
            whole = last_opening <= key_start
            pl.when(reached & whole)(functools.partial(tile, b, k0, 0, False))
            pl.when(reached & jnp.logical_not(whole))(functools.partial(tile, b, k0, 0, True))

    if last:
        dq_ref[...] = (dq_acc_ref[...] * SOFTMAX_SCALE).T.astype(BF16)
    else:
        dq_ref[0] = dq_acc_ref[...]

    @pl.when(head == pl.num_programs(0) - 1)
    def _():
        for b in range(blocks):
            dkv_refs[b][:, :HEAD_SIZE] = (acc_ref[b, :, :HEAD_SIZE] * SOFTMAX_SCALE).astype(dkv_refs[b].dtype)
            dkv_refs[b][:, HEAD_SIZE:] = acc_ref[b, :, HEAD_SIZE:].astype(dkv_refs[b].dtype)


def attention_step(shifts, first, last, rank, lengths, head_shift, q, do, second, kvs, dq):
    rows, width = q.shape
    heads = width // HEAD_SIZE
    blocks = len(shifts)
    smem = pl.BlockSpec(memory_space=pltpu.SMEM)
    head_block = pl.BlockSpec((rows, HEAD_SIZE), lambda h: (0, h))
    row_block = pl.BlockSpec((1, 1, rows), lambda h: (h, 0, 0))
    dq_block = pl.BlockSpec((1, HEAD_SIZE, rows), lambda h: (h, 0, 0))
    kv_block = pl.BlockSpec((rows, 2 * HEAD_SIZE), lambda h: (0, 0))
    in_specs = [smem, smem, smem, head_block, head_block, head_block if first else row_block]
    in_specs += [kv_block] * blocks + ([] if first else [dq_block])
    out_specs, out_shape = [], []
    if last:
        out_specs.append(head_block)
        out_shape.append(jax.ShapeDtypeStruct((rows, width), BF16))
    else:
        out_specs.append(dq_block)
        out_shape.append(jax.ShapeDtypeStruct((heads, HEAD_SIZE, rows), F32))
    if first:
        out_specs.append(row_block)
        out_shape.append(jax.ShapeDtypeStruct((heads, 1, rows), F32))
    for s in shifts:
        out_specs.append(kv_block)
        out_shape.append(jax.ShapeDtypeStruct((rows, 2 * HEAD_SIZE), F32 if s == 0 else BF16))
    pairs = heads * rows * rows * blocks
    return pl.pallas_call(
        functools.partial(attention_body, shifts, first, last),
        grid=(heads,),
        in_specs=in_specs,
        out_specs=out_specs,
        out_shape=out_shape,
        scratch_shapes=[
            pltpu.VMEM((blocks, rows, 2 * HEAD_SIZE), F32),
            pltpu.VMEM((blocks, HEAD_SIZE, rows), BF16),
            pltpu.VMEM((8, rows), jnp.int32),
            pltpu.VMEM((8, rows), F32),
            pltpu.VMEM((HEAD_SIZE, rows), F32),
        ],
        cost_estimate=pl.CostEstimate(
            flops=pairs * 10 * HEAD_SIZE, bytes_accessed=8 << 20, transcendentals=pairs
        ),
        compiler_params=vmem_params(),
        name="attention_" + "_".join(str(s) for s in shifts),
    )(rank, lengths, head_shift, q, do, second, *kvs, *([] if first else [dq]))


def product_body(count, x_ref, own_ref, *refs):
    parts, (out_ref, grad_ref) = refs[:count], refs[count:]

    @pl.when(pl.program_id(0) == 0)
    def _():
        total = own_ref[...]
        for part in parts:
            total = total + part[...].astype(F32)
        grad_ref[...] = total.astype(BF16)

    out_ref[0] = dot(grad_ref[...], x_ref[...], TN).astype(BF16)


def weight_product(features, own, parts, blocks):
    rows, width = features.shape
    cols = own.shape[1]
    whole = pl.BlockSpec((rows, cols), lambda d: (0, 0))
    return pl.pallas_call(
        functools.partial(product_body, len(parts)),
        grid=(blocks,),
        in_specs=[pl.BlockSpec((rows, width // blocks), lambda d: (0, d)), whole] + [whole] * len(parts),
        out_specs=pl.BlockSpec((1, cols, width // blocks), lambda d: (d, 0, 0)),
        out_shape=jax.ShapeDtypeStruct((blocks, cols, width // blocks), BF16),
        scratch_shapes=[pltpu.VMEM((rows, cols), BF16)],
        cost_estimate=pl.CostEstimate(
            flops=2 * rows * width * cols, bytes_accessed=12 << 20, transcendentals=0
        ),
        compiler_params=vmem_params(),
        name="weight_product",
    )(features, own, *parts)


def sum_body(x_ref, out_ref):
    total = x_ref[0].astype(F32)
    for n in range(1, x_ref.shape[0]):
        total = total + x_ref[n].astype(F32)
    width = out_ref.shape[2]
    for c in range(out_ref.shape[0]):
        out_ref[c] = total[:, c * width : (c + 1) * width].astype(BF16)


def sum_parts(x, blocks):
    n, rows, width = x.shape
    own = width // blocks
    per_step = 2
    return pl.pallas_call(
        sum_body,
        grid=(blocks // per_step,),
        in_specs=[pl.BlockSpec((n, rows, own * per_step), lambda c: (0, 0, c))],
        out_specs=pl.BlockSpec((per_step, rows, own), lambda c: (c, 0, 0)),
        out_shape=jax.ShapeDtypeStruct((blocks, rows, own), BF16),
        compiler_params=vmem_params(),
        name="part_sum",
    )(x)


def codes_body(parts_ref, dither_ref, out_ref):
    total = parts_ref[0].astype(F32)
    for n in range(1, parts_ref.shape[0]):
        total = total + parts_ref[n].astype(F32)
    for k in range(2):
        block = total[k * HEAD_SIZE : (k + 1) * HEAD_SIZE]
        largest = jnp.max(jnp.abs(block))
        scaled = 8.0 * block.T / (largest + 1e-06)
        out_ref[k] = scaled + (dither_ref[k].astype(F32) + 0.5) / 256.0


def weight_codes_of(parts, dither):
    return pl.pallas_call(
        codes_body,
        out_shape=jax.ShapeDtypeStruct(dither.shape, F32),
        compiler_params=vmem_params(),
        name="weight_codes",
    )(parts, dither)


def per_device(
    layer_input,
    queries,
    rotated_key_states,
    values,
    attention_out,
    output_grad,
    normalizer_shift,
    document_lengths,
    dither,
):
    context_size = lax.axis_size("context")
    dp_size = lax.axis_size("dp")
    rank = lax.axis_index("context").astype(jnp.int32).reshape(1)

    def send(x, by):
        pairs = [(i, (i + by) % context_size) for i in range(context_size)]
        return lax.ppermute(x, "context", pairs)

    own_kv = jnp.concatenate([rotated_key_states[0], values[0]], axis=1)
    kv = {0: own_kv}
    kv[1] = send(own_kv, 1)
    kv[6] = send(own_kv, -2)
    kv[2] = send(kv[1], 1)
    kv[5] = send(kv[6], -1)
    kv[3] = send(kv[2], 1)
    kv[4] = send(kv[5], -1)

    q, do = queries[0], output_grad[0]
    step = functools.partial(
        attention_step, rank=rank, lengths=document_lengths, head_shift=normalizer_shift, q=q, do=do
    )
    dq, delta, own = step((0,), True, False, second=attention_out[0], kvs=[kv[0]], dq=None)
    back = []
    groups = ((1,), (2, 6), (3, 5), (4,))
    for n, shifts in enumerate(groups):
        dq, *terms = step(
            shifts, False, n == len(groups) - 1, second=delta, kvs=[kv[s] for s in shifts], dq=dq
        )
        for s, term in zip(shifts, terms, strict=True):
            back.append(send(term, -s if s <= 4 else context_size - s))

    product = weight_product(layer_input[0], own, back, dp_size)
    parts = lax.all_to_all(product, "dp", 0, 0)
    parts = lax.all_to_all(sum_parts(parts, context_size), "context", 0, 0)
    weight_codes = weight_codes_of(parts, dither)
    return (dq[None], weight_codes)


def solution(mesh):
    placed = (
        P("dp", "context", None),
        P("dp", "context", "tensor"),
        P("dp", "context", "tensor"),
        P("dp", "context", "tensor"),
        P("dp", "context", "tensor"),
        P("dp", "context", "tensor"),
        P("tensor"),
        P("dp", None),
        P(None, ("dp", "context"), "tensor"),
    )
    return jax.shard_map(
        per_device,
        mesh=mesh,
        in_specs=placed,
        out_specs=(P("dp", "context", "tensor"), P(None, ("dp", "context"), "tensor")),
        check_vma=False,
    )
```

time: 805 us -> 208 us (0.26)
  waiting for transfers between devices: 621 us -> 24.2 us
  blocking collectives: 0 us -> 83.2 us
  starting transfers between devices: 0.37 us -> 62.6 us
  local copies, waits for them, and re-layouts: 61.3 us -> 4.99 us
  other arithmetic: 54.1 us -> 1 us
  Pallas kernels: 0 us -> 29.7 us
  matrix products: 26.3 us -> 0 us
  loops' own time: 21.8 us -> 0 us
  between operations: 13.9 us -> 0.7 us
    reduce_scatter x3 -> x0, waiting for transfers between devices: 546 us -> none  [the longest x1 328 us: per_device(): lax.psum_scatter(lax.dot_general(features, shared_grad, (((0,), (0,)), ((...]
    all_to_all x0 -> x2, blocking collectives: none -> 83.2 us  [the longest x1 59.9 us: per_device(): parts = lax.all_to_all(product, 'dp', 0, 0)]
    all_gather x2 -> x0, waiting for transfers between devices: 73.1 us -> none  [the longest x1 39 us: per_device(): value_piece = lax.all_gather(values, 'context', axis=1, tiled=True)[0]]
    ppermute x0 -> x12, starting transfers between devices: none -> 62.6 us  [send(): return lax.ppermute(x, 'context', pairs)]
    pallas_call x0 -> x8, Pallas kernels: none -> 29.7 us  [the longest x5 19.9 us: attention_step(): pl.pallas_call(functools.partial(attention_body, shifts, first, last), gr...]
    dot_general x11 -> x0, matrix products: 26.3 us -> none  [the longest x1 8.98 us: per_device(): lax.dot_general(features, shared_grad, (((0,), (0,)), ((), ())), preferre...]
    ppermute x0 -> x12, waiting for transfers between devices: none -> 24.2 us  [send(): return lax.ppermute(x, 'context', pairs)]
    slice x20 -> x0, local copies, waits for them, and re-layouts: 23 us -> none  [the longest x8 10.5 us: one_tile(): key_segment[tile_rows - 1] < query_segment[block, 0]]
  transfers between devices with their start and end apart: 5 -> 12, of which waited for: 5 -> 4; matrix products, arithmetic and copies ran while one was open for 1% -> 0% of each run, Pallas kernels for 0% -> 10%
where the time goes in v1:
time: 208 us; the launch traced here: 206 us
  blocking collectives  83.2 us (40%)
  starting transfers between devices  62.6 us (30%)
  Pallas kernels  29.7 us (14%)
  waiting for transfers between devices  24.2 us (12%)
  local copies, waits for them, and re-layouts  4.99 us (2%)
    ppermute x12, starting transfers between devices, send(): return lax.ppermute(x, 'context', pairs)  62.6 us
    all_to_all x1, blocking collectives, per_device(): parts = lax.all_to_all(product, 'dp', 0, 0)  59.9 us
    ppermute x12, waiting for transfers between devices, send(): return lax.ppermute(x, 'context', pairs)  24.2 us
    all_to_all x1, blocking collectives, per_device(): parts = lax.all_to_all(sum_parts(parts, context_size), 'context', 0, 0)  23.3 us
    pallas_call x5, Pallas kernels, attention_step(): pl.pallas_call(functools.partial(attention_body, shifts, first, last), gr...  19.9 us
    pallas_call x1, Pallas kernels, weight_product(): pl.pallas_call(functools.partial(product_body, len(parts)), grid=(blocks,...  7.72 us
    unnamed x12, local copies, waits for them, and re-layouts  4.99 us
  transfers between devices with their start and end apart: 12, of which 4 were waited for; matrix products, arithmetic and copies ran while one was open for 0% of the time, Pallas kernels for 10%

profile of v1, /device:TPU:4, one launch (start us, length us, event | category | flops | bytes accessed | tf_op | source)
XLA Modules:
  0.0 206.4 jit_solution(1756359908414125524)
XLA Ops:
  0.6 1.0 pad_maximum_fusion.refs_6_
  1.6 2.0 collective-permute-start.3
  3.6 5.4 %collective-permute-start = (bf16[512,256]{1,0:T(8,128)(2,1)S(1)}, bf16[512,256]{1,0:T(8,128)(2,1)S(1)}, u32[]{:S(2)}, u32[]{:S(2)}) collective-permute-start(bf16[512,256]{1,0:T(8,128)(2,1)S(1)} %pad_maximum_fusion.refs_6_), channel_id=1, source_target_pairs={{0,24},{4,28},{8,0},{12,4},{16,8},{20,12},{24,16},{28,20},{1,25},{... | collective-permute-start | bytes 786440 | tf_op jit(solution)/shard_map/ppermute | solution.py:259
  9.0 4.8 %collective-permute-done.3.refs_6_ = bf16[512,256]{1,0:T(8,128)(2,1)S(1)} collective-permute-done((bf16[512,256]{1,0:T(8,128)(2,1)S(1)}, bf16[512,256]{1,0:T(8,128)(2,1)S(1)}, u32[]{:S(2)}, u32[]{:S(2)}) %collective-permute-start.3) | collective-permute-done | bytes 262176 | tf_op jit(solution)/shard_map/ppermute | solution.py:259
  13.9 0.0 collective-permute-start.4
  13.9 0.0 copy-start.1
  13.9 1.2 copy-done.1
  15.1 0.0 copy-start.2
  15.1 1.2 copy-done.2
  16.3 0.0 copy-start.3
  16.3 1.2 copy-done.3
  17.5 0.0 copy-start.4
  17.6 0.7 copy-done.4
  18.2 0.0 copy-start.5
  18.2 0.7 copy-done.5
  18.9 8.3 %attention_0.1 = (f32[8,128,512]{2,1,0:T(8,128)S(1)}, f32[8,1,512]{2,1,0:T(1,128)S(1)}, f32[512,256]{1,0:T(8,128)S(1)}) custom-call(s32[1]{0:T(128)} %bitcast.refs_0_, s32[1,16]{1,0:T(1,128)S(1)} %copy-done.4, f32[8]{0:T(128)S(1)} %copy-done.5, bf16[512,1024]{1,0:T(8,128)(2,1)S(1)} %bitcast.9, bf16[512,1024]{1,0:T(8,128)(2,1)S(1)} %bitcast.14, ...), custom_call_target="tpu_custom_call" | custom-call | flops 2684354560 | bytes 8388608 | tf_op jit(solution)/shard_map/attention_0/pallas_call | solution.py:145
  27.2 2.2 %attention_1.1 = (f32[8,128,512]{2,1,0:T(8,128)S(1)}, bf16[512,256]{1,0:T(8,128)(2,1)S(1)}) custom-call(s32[1]{0:T(128)} %bitcast.refs_0_, s32[1,16]{1,0:T(1,128)S(1)} %copy-done.4, f32[8]{0:T(128)S(1)} %copy-done.5, bf16[512,1024]{1,0:T(8,128)(2,1)S(1)} %bitcast.10, bf16[512,1024]{1,0:T(8,128)(2,1)S(1)} %bitcast.15, ...), custom_call_target="tpu_custom_call" | custom-call | flops 2684354560 | bytes 8388608 | tf_op jit(solution)/shard_map/attention_1/pallas_call | solution.py:145
  29.4 11.8 %collective-permute-start.6 = (bf16[512,256]{1,0:T(8,128)(2,1)S(1)}, bf16[512,256]{1,0:T(8,128)(2,1)S(1)}, u32[]{:S(2)}, u32[]{:S(2)}) collective-permute-start(bf16[512,256]{1,0:T(8,128)(2,1)S(1)} %get-tuple-element.22), channel_id=1, source_target_pairs={{0,28},{4,0},{8,4},{12,8},{16,12},{20,16},{24,20},{28,24},{1,29},{... | collective-permute-start | bytes 786440 | tf_op jit(solution)/shard_map/ppermute | solution.py:259
  41.1 0.0 collective-permute-done.refs_7_
  41.1 0.1 collective-permute-start.1
  41.2 0.0 collective-permute-done.4.refs_6_
  41.2 1.9 collective-permute-start.5
  43.2 2.5 %attention_2_6.1 = (f32[8,128,512]{2,1,0:T(8,128)S(1)}, bf16[512,256]{1,0:T(8,128)(2,1)S(1)}, bf16[512,256]{1,0:T(8,128)(2,1)S(1)}) custom-call(s32[1]{0:T(128)} %bitcast.refs_0_, s32[1,16]{1,0:T(1,128)S(1)} %copy-done.4, f32[8]{0:T(128)S(1)} %copy-done.5, bf16[512,1024]{1,0:T(8,128)(2,1)S(1)} %bitcast.11, bf16[512,1024]{1,0:T(8,128)(2,1)S(1)} %bitcast.16, ...), custom_call_target="tpu_custom_call" | custom-call | flops 5368709120 | bytes 8388608 | tf_op jit(solution)/shard_map/attention_2_6/pallas_call | solution.py:145
  45.7 7.6 %collective-permute-start.7 = (bf16[512,256]{1,0:T(8,128)(2,1)S(1)}, bf16[512,256]{1,0:T(8,128)(2,1)S(1)}, u32[]{:S(2)}, u32[]{:S(2)}) collective-permute-start(bf16[512,256]{1,0:T(8,128)(2,1)S(1)} %get-tuple-element.23), channel_id=1, source_target_pairs={{0,24},{4,28},{8,0},{12,4},{16,8},{20,12},{24,16},{28,20},{1,25},{... | collective-permute-start | bytes 786440 | tf_op jit(solution)/shard_map/ppermute | solution.py:259
  53.3 0.0 collective-permute-start.8
  53.3 0.0 collective-permute-done.1.refs_7_
  53.3 10.9 %collective-permute-start.2 = (bf16[512,256]{1,0:T(8,128)(2,1)S(1)}, bf16[512,256]{1,0:T(8,128)(2,1)S(1)}, u32[]{:S(2)}, u32[]{:S(2)}) collective-permute-start(bf16[512,256]{1,0:T(8,128)(2,1)S(1)} %collective-permute-done.1.refs_7_), channel_id=1, source_target_pairs={{0,28},{4,0},{8,4},{12,8},{16,12},{20,16},{24,20},{28,24},{1,29},{... | collective-permute-start | bytes 786440 | tf_op jit(solution)/shard_map/ppermute | solution.py:259
  64.1 0.0 collective-permute-done.5.refs_6_
  64.1 2.5 %attention_3_5.1 = (f32[8,128,512]{2,1,0:T(8,128)S(1)}, bf16[512,256]{1,0:T(8,128)(2,1)S(1)}, bf16[512,256]{1,0:T(8,128)(2,1)S(1)}) custom-call(s32[1]{0:T(128)} %bitcast.refs_0_, s32[1,16]{1,0:T(1,128)S(1)} %copy-done.4, f32[8]{0:T(128)S(1)} %copy-done.5, bf16[512,1024]{1,0:T(8,128)(2,1)S(1)} %bitcast.12, bf16[512,1024]{1,0:T(8,128)(2,1)S(1)} %bitcast.17, ...), custom_call_target="tpu_custom_call" | custom-call | flops 5368709120 | bytes 8388608 | tf_op jit(solution)/shard_map/attention_3_5/pallas_call | solution.py:145
  66.6 5.1 %collective-permute-done.2.refs_6_ = bf16[512,256]{1,0:T(8,128)(2,1)S(1)} collective-permute-done((bf16[512,256]{1,0:T(8,128)(2,1)S(1)}, bf16[512,256]{1,0:T(8,128)(2,1)S(1)}, u32[]{:S(2)}, u32[]{:S(2)}) %collective-permute-start.2) | collective-permute-done | bytes 262176 | tf_op jit(solution)/shard_map/ppermute | solution.py:259
  71.7 4.5 %attention_4.1 = (bf16[512,1024]{1,0:T(8,128)(2,1)}, bf16[512,256]{1,0:T(8,128)(2,1)S(1)}) custom-call(s32[1]{0:T(128)} %bitcast.refs_0_, s32[1,16]{1,0:T(1,128)S(1)} %copy-done.4, f32[8]{0:T(128)S(1)} %copy-done.5, bf16[512,1024]{1,0:T(8,128)(2,1)S(1)} %bitcast.13, bf16[512,1024]{1,0:T(8,128)(2,1)S(1)} %bitcast.18, ...), custom_call_target="tpu_custom_call" | custom-call | flops 2684354560 | bytes 8388608 | tf_op jit(solution)/shard_map/attention_4/pallas_call | solution.py:145
  76.2 0.8 collective-permute-start.11
  77.0 5.0 %collective-permute-start.9 = (bf16[512,256]{1,0:T(8,128)(2,1)S(1)}, bf16[512,256]{1,0:T(8,128)(2,1)S(1)}, u32[]{:S(2)}, u32[]{:S(2)}) collective-permute-start(bf16[512,256]{1,0:T(8,128)(2,1)S(1)} %get-tuple-element.25), channel_id=1, source_target_pairs={{0,20},{4,24},{8,28},{12,0},{16,4},{20,8},{24,12},{28,16},{1,21},{... | collective-permute-start | bytes 786440 | tf_op jit(solution)/shard_map/ppermute | solution.py:259
  82.0 0.0 collective-permute-done.6.refs_0_
  82.0 17.1 %collective-permute-start.10 = (bf16[512,256]{1,0:T(8,128)(2,1)S(1)}, bf16[512,256]{1,0:T(8,128)(2,1)S(1)}, u32[]{:S(2)}, u32[]{:S(2)}) collective-permute-start(bf16[512,256]{1,0:T(8,128)(2,1)S(1)} %get-tuple-element.26), channel_id=1, source_target_pairs={{0,12},{4,16},{8,20},{12,24},{16,28},{20,0},{24,4},{28,8},{1,13},{... | collective-permute-start | bytes 786440 | tf_op jit(solution)/shard_map/ppermute | solution.py:259
  99.2 0.0 collective-permute-done.7.refs_1_
  99.2 0.0 collective-permute-done.8.refs_2_
  99.2 0.0 collective-permute-done.11.refs_5_
  99.2 12.8 %collective-permute-done.9.refs_3_ = bf16[512,256]{1,0:T(8,128)(2,1)S(1)} collective-permute-done((bf16[512,256]{1,0:T(8,128)(2,1)S(1)}, bf16[512,256]{1,0:T(8,128)(2,1)S(1)}, u32[]{:S(2)}, u32[]{:S(2)}) %collective-permute-start.9) | collective-permute-done | bytes 262176 | tf_op jit(solution)/shard_map/ppermute | solution.py:259
  112.0 1.4 collective-permute-done.10.refs_4_
  113.5 7.7 %weight_product.1 = bf16[8,256,1024]{2,1,0:T(8,128)(2,1)S(1)} custom-call(bf16[512,8192]{1,0:T(8,128)(2,1)} %bitcast.19, f32[512,256]{1,0:T(8,128)S(1)} %get-tuple-element.21.own_ref, bf16[512,256]{1,0:T(8,128)(2,1)S(1)} %collective-permute-done.6.refs_0_, bf16[512,256]{1,0:T(8,128)(2,1)S(1)} %collective-permute-done.7.refs_1_, ...), custom_call_target="tpu_custom_call" | custom-call | flops 2147483648 | bytes 12582912 | tf_op jit(solution)/shard_map/weight_product/pallas_call | solution.py:183
  121.2 59.9 %all_to_all.10.x_ref = bf16[8,256,1024]{2,1,0:T(8,128)(2,1)S(1)} all-to-all(bf16[8,256,1024]{2,1,0:T(8,128)(2,1)S(1)} %weight_product.1), channel_id=1, replica_groups=mesh['dp'=8,'context'=8,'tensor'=4] {'dp'}, dimensions={0} | all-to-all | bytes 8388608 | tf_op jit(solution)/shard_map/all_to_all | solution.py:285
  181.0 0.0 copy-start
  181.0 1.2 part_sum.1
  182.3 23.3 %all_to_all.11.parts_ref = bf16[8,256,128]{2,1,0:T(8,128)(2,1)S(1)} all-to-all(bf16[8,256,128]{2,1,0:T(8,128)(2,1)S(1)} %part_sum.1), channel_id=1, replica_groups=mesh['dp'=8,'context'=8,'tensor'=4] {'context'}, dimensions={0} | all-to-all | bytes 1048576 | tf_op jit(solution)/shard_map/all_to_all | solution.py:286
  205.6 0.0 copy-done
  205.6 0.9 weight_codes.1
Async XLA Ops:
  1.6 12.2 %collective-permute-start.3 = (bf16[512,256]{1,0:T(8,128)(2,1)S(1)}, bf16[512,256]{1,0:T(8,128)(2,1)S(1)}, u32[]{:S(2)}, u32[]{:S(2)}) collective-permute-start(bf16[512,256]{1,0:T(8,128)(2,1)S(1)} %pad_maximum_fusion.refs_6_), channel_id=1, source_target_pairs={{0,4},{4,8},{8,12},{12,16},{16,20},{20,24},{24,28},{28,0},{1,5},{5... | collective-permute-start | bytes 786440 | tf_op jit(solution)/shard_map/ppermute | solution.py:259
  3.6 37.5 %collective-permute-start = (bf16[512,256]{1,0:T(8,128)(2,1)S(1)}, bf16[512,256]{1,0:T(8,128)(2,1)S(1)}, u32[]{:S(2)}, u32[]{:S(2)}) collective-permute-start(bf16[512,256]{1,0:T(8,128)(2,1)S(1)} %pad_maximum_fusion.refs_6_), channel_id=1, source_target_pairs={{0,24},{4,28},{8,0},{12,4},{16,8},{20,12},{24,16},{28,20},{1,25},{... | collective-permute-start | bytes 786440 | tf_op jit(solution)/shard_map/ppermute | solution.py:259
  13.9 27.4 %collective-permute-start.4 = (bf16[512,256]{1,0:T(8,128)(2,1)S(1)}, bf16[512,256]{1,0:T(8,128)(2,1)S(1)}, u32[]{:S(2)}, u32[]{:S(2)}) collective-permute-start(bf16[512,256]{1,0:T(8,128)(2,1)S(1)} %collective-permute-done.3.refs_6_), channel_id=1, source_target_pairs={{0,4},{4,8},{8,12},{12,16},{16,20},{20,24},{24,28},{28,0},{1,5},{5... | collective-permute-start | bytes 786440 | tf_op jit(solution)/shard_map/ppermute | solution.py:259
  13.9 1.2 copy-start.1
  15.1 1.2 copy-start.2
  16.3 1.2 copy-start.3
  17.5 0.7 copy-start.4
  18.2 0.7 copy-start.5
  29.4 52.7 %collective-permute-start.6 = (bf16[512,256]{1,0:T(8,128)(2,1)S(1)}, bf16[512,256]{1,0:T(8,128)(2,1)S(1)}, u32[]{:S(2)}, u32[]{:S(2)}) collective-permute-start(bf16[512,256]{1,0:T(8,128)(2,1)S(1)} %get-tuple-element.22), channel_id=1, source_target_pairs={{0,28},{4,0},{8,4},{12,8},{16,12},{20,16},{24,20},{28,24},{1,29},{... | collective-permute-start | bytes 786440 | tf_op jit(solution)/shard_map/ppermute | solution.py:259
  41.1 12.1 %collective-permute-start.1 = (bf16[512,256]{1,0:T(8,128)(2,1)S(1)}, bf16[512,256]{1,0:T(8,128)(2,1)S(1)}, u32[]{:S(2)}, u32[]{:S(2)}) collective-permute-start(bf16[512,256]{1,0:T(8,128)(2,1)S(1)} %collective-permute-done.refs_7_), channel_id=1, source_target_pairs={{0,28},{4,0},{8,4},{12,8},{16,12},{20,16},{24,20},{28,24},{1,29},{... | collective-permute-start | bytes 786440 | tf_op jit(solution)/shard_map/ppermute | solution.py:259
  41.2 22.9 %collective-permute-start.5 = (bf16[512,256]{1,0:T(8,128)(2,1)S(1)}, bf16[512,256]{1,0:T(8,128)(2,1)S(1)}, u32[]{:S(2)}, u32[]{:S(2)}) collective-permute-start(bf16[512,256]{1,0:T(8,128)(2,1)S(1)} %collective-permute-done.4.refs_6_), channel_id=1, source_target_pairs={{0,4},{4,8},{8,12},{12,16},{16,20},{20,24},{24,28},{28,0},{1,5},{5... | collective-permute-start | bytes 786440 | tf_op jit(solution)/shard_map/ppermute | solution.py:259
  45.7 53.5 %collective-permute-start.7 = (bf16[512,256]{1,0:T(8,128)(2,1)S(1)}, bf16[512,256]{1,0:T(8,128)(2,1)S(1)}, u32[]{:S(2)}, u32[]{:S(2)}) collective-permute-start(bf16[512,256]{1,0:T(8,128)(2,1)S(1)} %get-tuple-element.23), channel_id=1, source_target_pairs={{0,24},{4,28},{8,0},{12,4},{16,8},{20,12},{24,16},{28,20},{1,25},{... | collective-permute-start | bytes 786440 | tf_op jit(solution)/shard_map/ppermute | solution.py:259
  53.3 45.9 %collective-permute-start.8 = (bf16[512,256]{1,0:T(8,128)(2,1)S(1)}, bf16[512,256]{1,0:T(8,128)(2,1)S(1)}, u32[]{:S(2)}, u32[]{:S(2)}) collective-permute-start(bf16[512,256]{1,0:T(8,128)(2,1)S(1)} %get-tuple-element.24), channel_id=1, source_target_pairs={{0,8},{4,12},{8,16},{12,20},{16,24},{20,28},{24,0},{28,4},{1,9},{5... | collective-permute-start | bytes 786440 | tf_op jit(solution)/shard_map/ppermute | solution.py:259
  53.3 18.4 %collective-permute-start.2 = (bf16[512,256]{1,0:T(8,128)(2,1)S(1)}, bf16[512,256]{1,0:T(8,128)(2,1)S(1)}, u32[]{:S(2)}, u32[]{:S(2)}) collective-permute-start(bf16[512,256]{1,0:T(8,128)(2,1)S(1)} %collective-permute-done.1.refs_7_), channel_id=1, source_target_pairs={{0,28},{4,0},{8,4},{12,8},{16,12},{20,16},{24,20},{28,24},{1,29},{... | collective-permute-start | bytes 786440 | tf_op jit(solution)/shard_map/ppermute | solution.py:259
  76.2 23.0 %collective-permute-start.11 = (bf16[512,256]{1,0:T(8,128)(2,1)S(1)}, bf16[512,256]{1,0:T(8,128)(2,1)S(1)}, u32[]{:S(2)}, u32[]{:S(2)}) collective-permute-start(bf16[512,256]{1,0:T(8,128)(2,1)S(1)} %get-tuple-element.27), channel_id=1, source_target_pairs={{0,16},{4,20},{8,24},{12,28},{16,0},{20,4},{24,8},{28,12},{1,17},{... | collective-permute-start | bytes 786440 | tf_op jit(solution)/shard_map/ppermute | solution.py:259
  77.0 35.0 %collective-permute-start.9 = (bf16[512,256]{1,0:T(8,128)(2,1)S(1)}, bf16[512,256]{1,0:T(8,128)(2,1)S(1)}, u32[]{:S(2)}, u32[]{:S(2)}) collective-permute-start(bf16[512,256]{1,0:T(8,128)(2,1)S(1)} %get-tuple-element.25), channel_id=1, source_target_pairs={{0,20},{4,24},{8,28},{12,0},{16,4},{20,8},{24,12},{28,16},{1,21},{... | collective-permute-start | bytes 786440 | tf_op jit(solution)/shard_map/ppermute | solution.py:259
  82.0 31.4 %collective-permute-start.10 = (bf16[512,256]{1,0:T(8,128)(2,1)S(1)}, bf16[512,256]{1,0:T(8,128)(2,1)S(1)}, u32[]{:S(2)}, u32[]{:S(2)}) collective-permute-start(bf16[512,256]{1,0:T(8,128)(2,1)S(1)} %get-tuple-element.26), channel_id=1, source_target_pairs={{0,12},{4,16},{8,20},{12,24},{16,28},{20,0},{24,4},{28,8},{1,13},{... | collective-permute-start | bytes 786440 | tf_op jit(solution)/shard_map/ppermute | solution.py:259
  181.0 24.5 %copy-start = (s32[2,128,128]{2,1,0:T(8,128)S(1)}, s32[2,128,128]{2,1,0:T(8,128)}, u32[]{:S(2)}) copy-start(s32[2,128,128]{2,1,0:T(8,128)} %dither_ref.1) | copy-start | bytes 393220
